TPU v7x, 256 devices: a whole 4x4x8 slice. The times are simulated.
256 devices in a mesh: col: 32 (over x, y, core), row: 8 (over z).
Axes of the slice: x: 4, y: 4, z: 8, core: 2. Of those that a mesh axis runs over, the one named last changes fastest.
Arguments:
- w_tiles: bfloat16 [256, 512, 512], P(('col', 'row')), may hold values from -0.03125 to 0.03125
- task_ab: int32 [256], P(('col', 'row')), may hold values from 0 to 3, as said below
- task_ef: int32 [256], P(('col', 'row')), may hold values from 0 to 7
- lam_pairs: bfloat16 [32768, 16384], P('row', 'col'), may hold values from -6 to 6
- other_terms: bfloat16 [2048, 16384], P('row', 'col'), may hold values from -6 to 6
- vir_pair: float32 [2048], P('row'), may hold values from 1 to 4
- occ_pair: float32 [16384], P('col'), may hold values from -3 to -1
Outputs:
- lam_new: bfloat16 [2048, 16384], P('row', 'col')
Inputs may be any that keep to these rules, and one draw needn't show every extreme that they name: Within one row group no pair (task_ab, task_ef) is listed twice.
All inputs are finite; a program needn't handle non-finite values.
Results may differ from a plain program's by a relative error of at most 0.001.
Values may be sent and summed in bfloat16 or wider, within the bound.
A program may use at most 64 MiB of HBM per device.

v0:
```python
import jax
import jax.numpy as jnp
from jax import lax
from jax.sharding import PartitionSpec as P

AB_T = 4


def add_tile(totals, tile_now, ab_id, ef_id, lam_blocks):
    block = lax.dynamic_index_in_dim(lam_blocks, ef_id, 0, keepdims=False)
    product = jnp.dot(tile_now, block, preferred_element_type=jnp.float32)
    current = lax.dynamic_index_in_dim(totals, ab_id, 0, keepdims=True)
    return lax.dynamic_update_index_in_dim(totals, current + product[None], ab_id, 0)


def body(w_tiles, task_ab, task_ef, lam_pairs, other_terms, vir_pair, occ_pair):
    tile_rows = w_tiles.shape[1]
    col_width = lam_pairs.shape[1]
    ef_count = lam_pairs.shape[0] // tile_rows
    lam_blocks = lam_pairs.reshape(ef_count, tile_rows, col_width)
    all_ab, all_ef = (
        lax.all_gather(task_ab, "col", axis=0, tiled=True),
        lax.all_gather(task_ef, "col", axis=0, tiled=True),
    )
    initial = jnp.zeros((AB_T, tile_rows, col_width), jnp.float32)
    totals = initial
    piece = lax.all_gather(w_tiles, "col", axis=0, tiled=True)
    piece_count = piece.shape[0]
    full_blocks = piece_count // 4

    def block_turn(turn, running):
        base = turn * 4
        tiles_here = lax.dynamic_slice_in_dim(piece, base, 4, 0)
        ab_here = lax.dynamic_slice_in_dim(all_ab, base, 4)
        ef_here = lax.dynamic_slice_in_dim(all_ef, base, 4)
        for inner in range(4):
            running = add_tile(
                running, tiles_here[inner], ab_here[inner], ef_here[inner], lam_blocks
            )
        return running

    totals = lax.fori_loop(0, full_blocks, block_turn, totals)
    ladder = totals
    ladder = ladder.reshape(AB_T * tile_rows, col_width)
    own_rows = other_terms.shape[0]
    summed = lax.psum(ladder, "row")
    owned = lax.dynamic_slice_in_dim(summed, lax.axis_index("row") * own_rows, own_rows, 0)
    combined = other_terms.astype(jnp.float32) + owned
    denominator = occ_pair[None, :] - vir_pair[:, None]
    return (combined / denominator).astype(jnp.bfloat16)


def solution(mesh):
    placed = (
        P(("col", "row"), None, None),
        P(("col", "row")),
        P(("col", "row")),
        P("row", "col"),
        P("row", "col"),
        P("row"),
        P("col"),
    )
    return jax.shard_map(
        body, mesh=mesh, in_specs=placed, out_specs=P("row", "col"), check_vma=False
    )
```

profile of v0, /device:TPU:1, one launch (start us, length us, event | category | flops | bytes accessed | tf_op | source)
XLA Modules:
  0.0 440.6 jit_solution(9258004406452614396)
XLA Ops:
  6.5 0.7 all-gather.2.cloned.1.call-update
  8.6 1.3 dynamic-slice
  9.9 0.8 dynamic-update-slice
  10.7 0.8 dynamic-update-slice.1
  11.5 14.4 %all-reduce.2 = (s32[32]{0:T(128)S(1)}, s32[32]{0:T(128)S(1)}) all-reduce(s32[32]{0:T(128)S(1)} %dynamic-update-slice, s32[32]{0:T(128)S(1)} %dynamic-update-slice.1), channel_id=1, replica_groups=mesh['col'=32,'row'=8] {'col'}, use_global_device_ids=true, to_apply=%add | all-reduce | flops 64 | bytes 512
  26.0 65.7 %all-gather.2.cloned.1.call-done = bf16[32,512,512]{2,1,0:T(8,128)(2,1)} async-done(((bf16[1,512,512]{2,1,0:T(8,128)(2,1)}), bf16[32,512,512]{2,1,0:T(8,128)(2,1)}) %all-gather.2.cloned.1.call-update) | async-done | bytes 16777232 | tf_op jit(solution)/shard_map/all_gather | solution.py:27
  91.7 2.5 broadcast_in_dim.33
  94.1 229.4 %while.13 = (s32[]{:T(128)}, f32[4,512,512]{2,1,0:T(8,128)}, s32[32]{0:T(128)S(1)}, bf16[32,512,512]{2,1,0:T(8,128)(2,1)}, s32[32]{0:T(128)S(1)}, /*index=5*/bf1...) while((s32[]{:T(128)}, f32[4,512,512]{2,1,0:T(8,128)}, ...), condition=%wide.region_1.2_spmd, body=%wide.region_0.1_spmd.sunk | while | flops 1074790400 | bytes 12583583 | solution.py:42
  97.0 0.7 fusion.36
  99.3 3.0 fusion.38
  106.0 3.0 fusion.39
  112.9 3.0 fusion.40
  119.8 3.0 fusion.41
  125.7 0.7 fusion.36
  128.0 3.0 fusion.38
  134.8 3.0 fusion.39
  141.7 3.0 fusion.40
  148.6 3.0 fusion.41
  154.4 0.7 fusion.36
  156.7 3.0 fusion.38
  163.4 3.0 fusion.39
  170.4 3.0 fusion.40
  177.3 3.0 fusion.41
  183.1 0.7 fusion.36
  185.4 3.0 fusion.38
  192.1 3.0 fusion.39
  199.1 3.0 fusion.40
  205.9 3.0 fusion.41
  211.7 0.7 fusion.36
  214.0 3.0 fusion.38
  220.8 3.0 fusion.39
  227.7 3.0 fusion.40
  234.5 3.0 fusion.41
  240.4 0.7 fusion.36
  242.7 3.0 fusion.38
  249.4 3.0 fusion.39
  256.4 3.0 fusion.40
  263.2 3.0 fusion.41
  271.4 3.0 fusion.38
  278.1 3.0 fusion.39
  285.1 3.0 fusion.40
  291.9 3.0 fusion.41
  300.0 3.0 fusion.38
  306.8 3.0 fusion.39
  313.7 3.0 fusion.40
  320.6 3.0 fusion.41
  323.6 108.3 %all-reduce.5.cloned.1.call-done = f32[2048,512]{1,0:T(8,128)} async-done(((f32[2048,512]{1,0:T(8,128)}), f32[2048,512]{1,0:T(8,128)}) %all-reduce.5.cloned.1.call-update) | async-done | bytes 4194320 | tf_op jit(solution)/shard_map/psum | solution.py:46
  431.9 1.9 divide_convert_fusion
  (37 shorter events, 7.8 us)
Async XLA Ops:
  6.5 85.1 %all-gather.2.cloned.1.call-start = ((), (), s32[]{:S(2)}) async-start(), calls=%async_computation | async-start | bytes 17301504 | tf_op jit(solution)/shard_map/all_gather | solution.py:27
  7.3 424.6 %all-reduce.5.cloned.1.call-start = ((), (), s32[]{:S(2)}) async-start(), calls=%async_computation.1 | async-start | bytes 8388608 | tf_op jit(solution)/shard_map/psum | solution.py:46
  323.5 108.3 %copy-start = (bf16[256,512]{1,0:T(8,128)(2,1)S(1)}, bf16[256,512]{1,0:T(8,128)(2,1)}, u32[]{:S(2)}) copy-start(bf16[256,512]{1,0:T(8,128)(2,1)} %param.13) | copy-start | bytes 786436
  323.5 108.3 %copy-start.1 = (f32[512]{0:T(512)S(1)}, f32[512]{0:T(512)}, u32[]{:S(2)}) copy-start(f32[512]{0:T(512)} %param.15) | copy-start | bytes 6148
  323.5 108.3 %copy-start.2 = (f32[256]{0:T(256)S(1)}, f32[256]{0:T(256)}, u32[]{:S(2)}) copy-start(f32[256]{0:T(256)} %param.14) | copy-start | bytes 3076
Sparse Core Ops, SparseCore 0:
  9.9 81.7 all-gather.1
  323.7 108.1 all-reduce.4
where the time goes:
time: 443 us; the launch traced here: 441 us
  waiting for transfers between devices  175 us (40%)
  loops' own time  122 us (28%)
  matrix products  95.6 us (22%)
  local copies, waits for them, and re-layouts  17.2 us (4%)
  between operations  14.7 us (3%)
  blocking collectives  14.4 us (3%)
    another operation x1, loops' own time, body(): totals = lax.fori_loop(0, full_blocks, block_turn, totals)  122 us
    psum x1, waiting for transfers between devices, body(): summed = lax.psum(ladder, 'row')  108 us
    dot_general x32, matrix products, add_tile(): product = jnp.dot(tile_now, block, preferred_element_type=jnp.float32)  95.6 us
    all_gather x1, waiting for transfers between devices, body(): piece = lax.all_gather(w_tiles, 'col', axis=0, tiled=True)  65.7 us
    unnamed x1, blocking collectives  14.4 us
  transfers between devices with their start and end apart: 2, of which 2 were waited for; matrix products, arithmetic and copies ran while one was open for 1% of the time, Pallas kernels for 0%

commit v1 on v0

v1 whole, which is shorter than its diff:
```python
import jax
import jax.numpy as jnp
from jax import lax
from jax.experimental import pallas as pl
from jax.experimental.pallas import tpu as pltpu
from jax.sharding import PartitionSpec as P

TILE = 512
AB_T = 4
EF_T = 8
NX = NY = 4
NZ = 8
NK = 8
R = 16
W2 = 512

S_1A, S_1B, S_2A, S_2B, S_MM, S_H1, S_H2, S_H3, S_FIN = range(9)


def kernel(ab_ref, ef_ref, w_ref, lam_ref, other_ref, vir_ref, occ_ref, out_ref, *scratch):
    land = scratch[:NK]
    part = scratch[NK : 2 * NK]
    (
        lam_v, lhs, hop0, hop1, hop2, last, swap, other_v, vir_v, occ_v, vir_t,
        ids, inv_v, inv_s,
        in_sem, start_send, start_recv, id_send, id_recv, g_send, g_recv,
        h_send, h_recv, l_send, l_recv, s_send, s_recv,
    ) = scratch[2 * NK :]

    col = lax.axis_index("col")
    z = lax.axis_index("row")
    core = lax.rem(col, 2)
    y = lax.rem(col // 2, NY)
    x = col // (2 * NY)

    def dev(xx, yy, cc, zz):
        return ((xx * NY + yy) * 2 + cc, zz)

    def step4(v, d):
        return lax.rem(v + (4 + d), 4)

    def stepz(v, d):
        return lax.rem(v + (NZ + d), NZ)

    def remote(src, dst, send, recv, device):
        return pltpu.make_async_remote_copy(
            src_ref=src, dst_ref=dst, send_sem=send, recv_sem=recv,
            device_id=device, device_id_type=pl.DeviceIdType.MESH,
        )

    partner = dev(x, y, 1 - core, z)
    prime = (x, y)
    second = (y, x)
    around1 = (
        {d: dev(step4(x, d), y, core, z) for d in (1, -1)},
        {d: dev(x, step4(y, d), core, z) for d in (1, -1)},
    )
    around2 = (around1[1], around1[0])
    updown = {d: [dev(x, y, j, stepz(z, d)) for j in (0, 1)] for d in (1, -1)}
    updown_same = {d: dev(x, y, core, stepz(z, d)) for d in (1, -1)}

    def slot(g, s, p):
        return g * 16 + s * 4 + p

    my_slot = core * 16 + jnp.where(core == 0, y * 4 + x, x * 4 + y)

    barrier = pltpu.get_barrier_semaphore()
    greeted = [partner]
    for d in (1, -1):
        greeted += [around1[0][d], around1[1][d], updown[d][0], updown[d][1]]
    for who in greeted:
        pl.semaphore_signal(barrier, inc=1, device_id=who, device_id_type=pl.DeviceIdType.MESH)

    local_w = [
        pltpu.make_async_copy(w_ref.at[:, core, k], land[k].at[my_slot], in_sem.at[k])
        for k in range(NK)
    ]
    for c in local_w:
        c.start()
    local_lam = pltpu.make_async_copy(lam_ref, lam_v.at[core], in_sem.at[NK])
    local_lam.start()
    small = [
        pltpu.make_async_copy(vir_ref, vir_v, in_sem.at[NK + 1]),
        pltpu.make_async_copy(occ_ref, occ_v, in_sem.at[NK + 2]),
        pltpu.make_async_copy(other_ref, other_v, in_sem.at[NK + 3]),
    ]
    for c in small:
        c.start()

    code = ab_ref[0] * EF_T + ef_ref[0]
    lane = lax.broadcasted_iota(jnp.int32, (8, 128), 1)
    ids[y, x, core] = jnp.where(lane == code, my_slot, 0)

    pl.semaphore_wait(barrier, len(greeted))

    sent = []

    def go(copy):
        copy.start()
        sent.append(copy)
        return copy

    start_w = [
        go(remote(w_ref.at[:, 1 - core, k], land[k].at[my_slot], start_send.at[k], start_recv.at[k], partner))
        for k in range(NK)
    ]
    id0 = go(remote(ids.at[y, x, core], ids.at[y, x, core], id_send.at[0], id_recv.at[0], partner))
    start_lam = go(remote(lam_ref, lam_v.at[core], start_send.at[NK], start_recv.at[NK], partner))

    moves = {}

    def gather_copy(k, g, stage, d):
        s, p = second[g], prime[g]
        ref = land[k]
        n = 0 if d == 1 else 1
        if stage == 0:
            view, who = ref.at[slot(g, s, p)], around1[g][d]
        elif stage == 1:
            view, who = ref.at[slot(g, s, step4(p, -d)), n], around1[g][d]
        elif stage == 2:
            view, who = ref.at[pl.ds(slot(g, s, 0), 4)], around2[g][d]
        else:
            view, who = ref.at[pl.ds(slot(g, step4(s, -d), 2 * n), 2)], around2[g][d]
        moves[k, g, stage, d] = go(
            remote(view, view, g_send.at[k, g, stage, n], g_recv.at[k, g, stage, n], who)
        )

    def stage_1a(k):
        local_w[k].wait()
        start_w[k].wait_recv()
        for g in (0, 1):
            for d in (1, -1):
                gather_copy(k, g, 0, d)

    def stage_next(k, stage):
        for g in (0, 1):
            for d in (1, -1):
                moves[k, g, stage - 1, d].wait_recv()
                if stage in (1, 3):
                    gather_copy(k, g, stage, d)
            if stage == 2:
                for d in (1, -1):
                    gather_copy(k, g, stage, d)

    id_moves = {}

    def id_copy(n, view, who):
        id_moves[n] = go(remote(view, view, id_send.at[n], id_recv.at[n], who))

    def id_stage(s):
        if s == 0:
            id0.wait_recv()
            id_copy(1, ids.at[y, x], around1[0][1])
            id_copy(2, ids.at[y, x], around1[0][-1])
        elif s == 1:
            id_moves[1].wait_recv()
            id_copy(3, ids.at[y, step4(x, -1)], around1[0][1])
            id_moves[2].wait_recv()
        elif s == 2:
            id_moves[3].wait_recv()
            id_copy(4, ids.at[y], around1[1][1])
            id_copy(5, ids.at[y], around1[1][-1])
        elif s == 3:
            id_moves[4].wait_recv()
            id_copy(6, ids.at[step4(y, -1)], around1[1][1])
            id_moves[5].wait_recv()
        else:
            id_moves[6].wait_recv()
            inv_v[...] = jnp.max(ids[...], axis=(0, 1, 2))
            get = pltpu.make_async_copy(inv_v, inv_s, in_sem.at[NK + 4])
            get.start()
            for c in small:
                c.wait()
            for n in (0, 1):
                row = jnp.broadcast_to(vir_v[n : n + 1, :], (128, 128))
                vir_t[n * 128 : (n + 1) * 128, :] = row.T
            get.wait()
            local_lam.wait()
            start_lam.wait_recv()

    def multiply(k):
        for g in (0, 1):
            for d in (1, -1):
                moves[k, g, 3, d].wait_recv()

        def order(ab, carry):
            for ef in range(EF_T):
                tile = land[k][inv_s[0, ab * EF_T + ef]]
                lhs[pl.ds(pl.multiple_of(ab * (2 * R), 2 * R), 2 * R), ef * TILE : (ef + 1) * TILE] = tile.reshape(2 * R, TILE)
            return carry

        lax.fori_loop(0, AB_T, order, 0)

        def half(j, carry):
            for q in range(W2 // 256):
                cols = slice(q * 256, (q + 1) * 256)
                product = jnp.dot(lhs[...], lam_v[j, :, cols], preferred_element_type=jnp.float32)
                part[k][j, :, :, cols] = product.reshape(NZ, R, 256)
            return carry

        lax.fori_loop(0, 2, half, 0)
        far = stepz(z, 4)
        for n, d in enumerate((1, -1)):
            moves[k, "h0", d] = go(
                remote(part[k].at[n, far], hop0.at[k, n], h_send.at[k, 0, n], h_recv.at[k, 0, n], updown_same[d])
            )
        moves[k, "swap"] = go(
            remote(part[k].at[1 - core, z], swap.at[k], s_send.at[k], s_recv.at[k], partner)
        )

    def hop_1(k):
        for n, d in enumerate((1, -1)):
            moves[k, "h0", d].wait_recv()
            block = stepz(z, 3 * d)
            part[k][n, block] = part[k][n, block] + hop0[k, n]
            moves[k, "h1", d] = go(
                remote(part[k].at[:, block], hop1.at[k, n], h_send.at[k, 1, n], h_recv.at[k, 1, n], updown_same[d])
            )

    def hop_2(k):
        for n, d in enumerate((1, -1)):
            moves[k, "h1", d].wait_recv()
            block = stepz(z, 2 * d)
            part[k][:, block] = part[k][:, block] + hop1[k, n]
            moves[k, "h2", d] = go(
                remote(part[k].at[:, block], hop2.at[k, n], h_send.at[k, 2, n], h_recv.at[k, 2, n], updown_same[d])
            )

    def hop_3(k):
        for n, d in enumerate((1, -1)):
            moves[k, "h2", d].wait_recv()
            block = stepz(z, d)
            for j in (0, 1):
                part[k][j, block] = part[k][j, block] + hop2[k, n, j]
                moves[k, "h3", d, j] = go(
                    remote(
                        part[k].at[j, block], last.at[k, n, core],
                        l_send.at[k, n, j], l_recv.at[k, n, core], updown[d][j],
                    )
                )

    def finish(k):
        moves[k, "swap"].wait_recv()
        for n in (0, 1):
            for j in (0, 1):
                here = last.at[k, n, j]
                remote(here, here, l_send.at[k, n, j], l_recv.at[k, n, j], partner).wait_recv()
        for who, own in ((core, part[k][core, z]), (1 - core, swap[k])):
            rows = pl.ds(pl.multiple_of(who * 128 + k * R, R), R)
            ladder = own + last[k, 0, who] + last[k, 1, who]
            v = vir_t[rows, :]
            den = occ_v[...] - jnp.concatenate([v] * (W2 // 128), axis=1)
            out_ref[rows, :] = ((other_v[rows, :].astype(jnp.float32) + ladder) / den).astype(jnp.bfloat16)

    for step in range(NK + S_FIN):
        def at(offset):
            k = step - offset
            return k if 0 <= k < NK else None

        k = at(S_1A)
        if k is not None:
            stage_1a(k)
        if step <= 4:
            id_stage(step)
        for offset, stage in ((S_1B, 1), (S_2A, 2), (S_2B, 3)):
            k = at(offset)
            if k is not None:
                stage_next(k, stage)
        for offset, run in ((S_MM, multiply), (S_H1, hop_1), (S_H2, hop_2), (S_H3, hop_3), (S_FIN, finish)):
            k = at(offset)
            if k is not None:
                run(k)

    for c in sent:
        c.wait_send()


def body(w_tiles, task_ab, task_ef, lam_pairs, other_terms, vir_pair, occ_pair):
    w = w_tiles.reshape(2, 2, NK, R, TILE)
    anyspace = pl.BlockSpec(memory_space=pl.ANY)
    smem = pl.BlockSpec(memory_space=pltpu.SMEM)
    f32, bf16 = jnp.float32, jnp.bfloat16
    dma = pltpu.SemaphoreType.DMA
    scratch = [pltpu.VMEM((32, 2, R, TILE), bf16) for _ in range(NK)]
    scratch += [pltpu.VMEM((2, NZ, R, W2), f32) for _ in range(NK)]
    scratch += [
        pltpu.VMEM((2, EF_T * TILE, W2), bf16),
        pltpu.VMEM((AB_T * 2 * R, EF_T * TILE), bf16),
        pltpu.VMEM((NK, 2, R, W2), f32),
        pltpu.VMEM((NK, 2, 2, R, W2), f32),
        pltpu.VMEM((NK, 2, 2, R, W2), f32),
        pltpu.VMEM((NK, 2, 2, R, W2), f32),
        pltpu.VMEM((NK, R, W2), f32),
        pltpu.VMEM((256, W2), bf16),
        pltpu.VMEM((2, 128), f32),
        pltpu.VMEM((1, W2), f32),
        pltpu.VMEM((256, 128), f32),
        pltpu.VMEM((NY, NX, 2, 8, 128), jnp.int32),
        pltpu.VMEM((8, 128), jnp.int32),
        pltpu.SMEM((8, 128), jnp.int32),
        dma((NK + 5,)),
        dma((NK + 1,)), dma((NK + 1,)),
        dma((7,)), dma((7,)),
        dma((NK, 2, 4, 2)), dma((NK, 2, 4, 2)),
        dma((NK, 3, 2)), dma((NK, 3, 2)),
        dma((NK, 2, 2)), dma((NK, 2, 2)),
        dma((NK,)), dma((NK,)),
    ]
    return pl.pallas_call(
        kernel,
        out_shape=jax.ShapeDtypeStruct((256, W2), bf16),
        in_specs=[smem, smem] + [anyspace] * 5,
        out_specs=pl.BlockSpec(memory_space=pltpu.VMEM),
        scratch_shapes=scratch,
        compiler_params=pltpu.CompilerParams(
            collective_id=0, has_side_effects=True, vmem_limit_bytes=48 * 1024 * 1024
        ),
        cost_estimate=pl.CostEstimate(
            flops=2 * 2048 * 4096 * 512, bytes_accessed=6 * 1024 * 1024, transcendentals=0
        ),
    )(task_ab, task_ef, w, lam_pairs, other_terms, vir_pair.reshape(2, 128), occ_pair.reshape(1, W2))


def solution(mesh):
    placed = (
        P(("col", "row"), None, None),
        P(("col", "row")),
        P(("col", "row")),
        P("row", "col"),
        P("row", "col"),
        P("row"),
        P("col"),
    )
    return jax.shard_map(
        body, mesh=mesh, in_specs=placed, out_specs=P("row", "col"), check_vma=False
    )
```

time: 443 us -> 96.2 us (0.22)
  waiting for transfers between devices: 175 us -> 0 us
  loops' own time: 122 us -> 0 us
  matrix products: 95.6 us -> 0 us
  Pallas kernels: 0 us -> 88.4 us
  blocking collectives: 14.4 us -> 0 us
  between operations: 14.7 us -> 1.32 us
  local copies, waits for them, and re-layouts: 17.2 us -> 6.24 us
    another operation x1 -> x0, loops' own time: 122 us -> none  [body(): totals = lax.fori_loop(0, full_blocks, block_turn, totals)]
    psum x1 -> x0, waiting for transfers between devices: 108 us -> none  [body(): summed = lax.psum(ladder, 'row')]
    dot_general x32 -> x0, matrix products: 95.6 us -> none  [add_tile(): product = jnp.dot(tile_now, block, preferred_element_type=jnp.float32)]
    pallas_call x0 -> x1, Pallas kernels: none -> 88.4 us  [body(): pl.pallas_call(kernel, out_shape=jax.ShapeDtypeStruct((256, W2), bf16), i...]
    all_gather x1 -> x0, waiting for transfers between devices: 65.7 us -> none  [body(): piece = lax.all_gather(w_tiles, 'col', axis=0, tiled=True)]
    unnamed x1 -> x0, blocking collectives: 14.4 us -> none
    slice x16 -> x0, local copies, waits for them, and re-layouts: 10.6 us -> none  [the longest x8 5.35 us: block_turn(): ab_here[inner]]
  transfers between devices with their start and end apart: 2 -> 0, of which waited for: 2 -> 0; matrix products, arithmetic and copies ran while one was open for 1% -> 0% of each run, Pallas kernels for 0% -> 0%
where the time goes in v1:
time: 96.2 us; the launch traced here: 96 us
  Pallas kernels  88.4 us (92%)
  local copies, waits for them, and re-layouts  6.24 us (6%)
  between operations  1.32 us (1%)
    pallas_call x1, Pallas kernels, body(): pl.pallas_call(kernel, out_shape=jax.ShapeDtypeStruct((256, W2), bf16), i...  88.4 us
    unnamed x11, local copies, waits for them, and re-layouts  6.24 us

profile of v1, /device:TPU:1, one launch (start us, length us, event | category | flops | bytes accessed | tf_op | source)
XLA Modules:
  0.0 96.0 jit_solution(7216024707546970077)
XLA Ops:
  1.3 0.0 copy-start
  1.3 2.2 %copy-done = bf16[4096,512]{1,0:T(8,128)(2,1)S(1)} copy-done((bf16[4096,512]{1,0:T(8,128)(2,1)S(1)}, bf16[4096,512]{1,0:T(8,128)(2,1)}, u32[]{:S(2)}) %copy-start) | copy-done | bytes 4194328
  3.5 0.0 copy-start.1
  3.5 1.0 %copy-done.1 = bf16[1,512,512]{2,1,0:T(8,128)(2,1)S(1)} copy-done((bf16[1,512,512]{2,1,0:T(8,128)(2,1)S(1)}, bf16[1,512,512]{2,1,0:T(8,128)(2,1)}, u32[]{:S(2)}) %copy-start.1) | copy-done | bytes 524312
  4.5 0.0 copy-start.2
  4.5 0.9 copy-done.2
  5.5 0.0 copy-start.3
  5.5 0.7 copy-done.3
  6.2 0.0 copy-start.4
  6.2 0.7 copy-done.4
  6.8 88.4 %shard_map.73 = bf16[256,512]{1,0:T(8,128)(2,1)S(1)} custom-call(s32[1]{0:T(128)S(6)} %copy.9.ab_ref, s32[1]{0:T(128)S(6)} %copy.10.ef_ref, bf16[2,2,8,16,512]{4,3,2,1,0:T(8,128)(2,1)S(1)} %bitcast.3, bf16[4096,512]{1,0:T(8,128)(2,1)S(1)} %copy-done, bf16[256,512]{1,0:T(8,128)(2,1)S(1)} %copy-done.2, f32[2,128]{1,0:T(2,128)S(1)} %bitcast.5, f32[1,512]{1,0:T(1,128)S(1)} %bitcast.4), custom_call_target="tpu_custom_call" | custom-call | flops 8589934592 | bytes 6291456 | tf_op jit(solution)/shard_map/pallas_call | solution.py:309
  95.3 0.7 copy.11
Async XLA Ops:
  1.3 2.2 %copy-start = (bf16[4096,512]{1,0:T(8,128)(2,1)S(1)}, bf16[4096,512]{1,0:T(8,128)(2,1)}, u32[]{:S(2)}) copy-start(bf16[4096,512]{1,0:T(8,128)(2,1)} %lam_ref.1) | copy-start | bytes 12582916
  3.5 1.0 %copy-start.1 = (bf16[1,512,512]{2,1,0:T(8,128)(2,1)S(1)}, bf16[1,512,512]{2,1,0:T(8,128)(2,1)}, u32[]{:S(2)}) copy-start(bf16[1,512,512]{2,1,0:T(8,128)(2,1)} %param.7) | copy-start | bytes 1572868
  4.5 0.9 copy-start.2
  5.5 0.7 copy-start.3
  6.2 0.7 copy-start.4

commit v2 on v1

v2 whole, which is shorter than its diff:
```python
import jax
import jax.numpy as jnp
from jax import lax
from jax.experimental import pallas as pl
from jax.experimental.pallas import tpu as pltpu
from jax.sharding import PartitionSpec as P

TILE = 512
AB_T = 4
EF_T = 8
NX = NY = 4
NZ = 8
NK = 8
R = 16
W2 = 512
VMEM = 63 * 1024 * 1024

S_1A, S_1B, S_2A, S_2B, S_MM, S_H1, S_H2, S_H3, S_FIN = range(9)


def timetable():
    table = {}

    def put(step, stage, k):
        table.setdefault((step, stage), []).append(k)

    for k in range(NK):
        if k == 0:
            times = {S_1A: 0, S_2A: 1, S_MM: 2, S_H1: 3, S_H2: 4, S_H3: 5, S_FIN: 6}
        else:
            times = {stage: k - 1 + stage for stage in range(9)}
        for stage, step in times.items():
            put(step, stage, k)
    return table


def kernel(ab_ref, ef_ref, w_ref, lam_ref, other_ref, vir_ref, occ_ref, out_ref, *scratch):
    land = scratch[:NK]
    part = scratch[NK : 2 * NK]
    (
        w_v, lam_v, lhs, hop0, hop1, hop2, last, swap, other_v, vir_v, occ_v, vir_t,
        ids, inv_v, inv_s,
        in_sem, lam_send, lam_recv, id_send, id_recv, g_send, g_recv,
        h_send, h_recv, s_send, s_recv,
    ) = scratch[2 * NK :]

    col = lax.axis_index("col")
    z = lax.axis_index("row")
    core = lax.rem(col, 2)
    y = lax.rem(col // 2, NY)
    x = col // (2 * NY)

    def dev(xx, yy, cc, zz):
        return ((xx * NY + yy) * 2 + cc, zz)

    def step4(v, d):
        return lax.rem(v + (4 + d), 4)

    def stepz(v, d):
        return lax.rem(v + (NZ + d), NZ)

    def remote(src, dst, send, recv, device):
        return pltpu.make_async_remote_copy(
            src_ref=src, dst_ref=dst, send_sem=send, recv_sem=recv,
            device_id=device, device_id_type=pl.DeviceIdType.MESH,
        )

    partner = dev(x, y, 1 - core, z)
    prime = (x, y)
    second = (y, x)
    near = {
        (axis, d, j): dev(step4(x, d), y, j, z) if axis == 0 else dev(x, step4(y, d), j, z)
        for axis in (0, 1) for d in (1, -1, 2) for j in (0, 1)
    }

    def around(axis, d, j):
        if axis == 0:
            return dev(step4(x, d), y, j, z)
        return dev(x, step4(y, d), j, z)

    updown = {d: [dev(x, y, j, stepz(z, d)) for j in (0, 1)] for d in (1, -1)}

    get_w = pltpu.make_async_copy(w_ref, w_v, in_sem.at[0])
    get_w.start()
    get_lam = pltpu.make_async_copy(lam_ref, lam_v.at[core], in_sem.at[1])
    get_lam.start()
    small = [
        pltpu.make_async_copy(vir_ref, vir_v, in_sem.at[2]),
        pltpu.make_async_copy(occ_ref, occ_v, in_sem.at[3]),
        pltpu.make_async_copy(other_ref, other_v, in_sem.at[4]),
    ]
    for c in small:
        c.start()

    barrier = pltpu.get_barrier_semaphore()
    greeted = [partner] + list(near.values()) + updown[1] + updown[-1]
    for who in greeted:
        pl.semaphore_signal(barrier, inc=1, device_id=who, device_id_type=pl.DeviceIdType.MESH)

    my_slot = core * 16 + jnp.where(core == 0, y * 4 + x, x * 4 + y)
    my_id = (y * 4 + x) * 2 + core
    code = ab_ref[0] * EF_T + ef_ref[0]
    lane = lax.broadcasted_iota(jnp.int32, (8, 128), 1)
    ids[my_id] = jnp.where(lane == code, my_slot, 0)
    get_w.wait()
    for k in range(NK):
        land[k][my_slot] = w_v[:, core, k]

    pl.semaphore_wait(barrier, len(greeted))

    sent = []

    def mine_along(d, j):
        xx = jnp.where(core == 0, step4(x, d), x)
        yy = jnp.where(core == 0, y, step4(y, d))
        return dev(xx, yy, j, z)

    def stage_1a(k):
        send, recv = g_send.at[k, 0], g_recv.at[k, 0]
        hops = (1, -1, 2) if k == 0 else (1, -1)
        for d in hops:
            for j in (0, 1):
                remote(w_v.at[:, j, k], land[k].at[my_slot], send, recv, mine_along(d, j)).start()
        remote(w_v.at[:, 1 - core, k], land[k].at[my_slot], send, recv, partner).start()
        expect(land[k].at[pl.ds(0, 2 * len(hops) + 1)], send, recv, (k, 0))

    arrivals = {}

    def expect(view, send, recv, key):
        both = remote(view, view, send, recv, partner)
        arrivals[key] = both
        sent.append(both)

    def slot(g, s, p):
        return g * 16 + s * 4 + p

    def stage_1b(k):
        arrivals[k, 0].wait_recv()
        send, recv = g_send.at[k, 1], g_recv.at[k, 1]
        for g in (0, 1):
            for n, d in enumerate((1, -1)):
                view = land[k].at[slot(g, second[g], step4(prime[g], -d)), n]
                remote(view, view, send, recv, around(g, d, core)).start()
        expect(land[k].at[pl.ds(0, 2)], send, recv, (k, 1))

    def stage_2a(k):
        arrivals[k, 0 if k == 0 else 1].wait_recv()
        send, recv = g_send.at[k, 2], g_recv.at[k, 2]
        hops = (1, -1, 2) if k == 0 else (1, -1)
        for g in (0, 1):
            view = land[k].at[pl.ds(slot(g, second[g], 0), 4)]
            for d in hops:
                remote(view, view, send, recv, around(1 - g, d, core)).start()
        expect(land[k].at[pl.ds(0, 8 * len(hops))], send, recv, (k, 2))

    def stage_2b(k):
        arrivals[k, 2].wait_recv()
        send, recv = g_send.at[k, 3], g_recv.at[k, 3]
        for g in (0, 1):
            for n, d in enumerate((1, -1)):
                view = land[k].at[pl.ds(slot(g, step4(second[g], -d), 2 * n), 2)]
                remote(view, view, send, recv, around(1 - g, d, core)).start()
        expect(land[k].at[pl.ds(0, 8)], send, recv, (k, 3))

    def ids_first():
        for d in (1, -1, 2):
            for j in (0, 1):
                remote(ids.at[my_id], ids.at[my_id], id_send.at[0], id_recv.at[0], around(0, d, j)).start()
        remote(ids.at[my_id], ids.at[my_id], id_send.at[0], id_recv.at[0], partner).start()
        expect(ids.at[pl.ds(0, 7)], id_send.at[0], id_recv.at[0], "id0")

    def ids_second():
        arrivals["id0"].wait_recv()
        view = ids.at[pl.ds(y * 8, 8)]
        for d in (1, -1, 2):
            remote(view, view, id_send.at[1], id_recv.at[1], around(1, d, core)).start()
        expect(ids.at[pl.ds(0, 24)], id_send.at[1], id_recv.at[1], "id1")

    def ids_done():
        arrivals["id1"].wait_recv()
        inv_v[...] = jnp.max(ids[...], axis=0)
        get = pltpu.make_async_copy(inv_v, inv_s, in_sem.at[5])
        get.start()
        for c in small:
            c.wait()
        for n in (0, 1):
            row = jnp.broadcast_to(vir_v[n : n + 1, :], (128, 128))
            vir_t[n * 128 : (n + 1) * 128, :] = row.T
        get.wait()
        get_lam.wait()
        give_lam.wait_recv()

    def multiply(k):
        arrivals[k, 2 if k == 0 else 3].wait_recv()

        def order(ab, carry):
            for ef in range(EF_T):
                tile = land[k][inv_s[0, ab * EF_T + ef]]
                rows = pl.ds(pl.multiple_of(ab * (2 * R), 2 * R), 2 * R)
                lhs[rows, ef * TILE : (ef + 1) * TILE] = tile.reshape(2 * R, TILE)
            return carry

        lax.fori_loop(0, AB_T, order, 0)

        def half(j, carry):
            for q in range(W2 // 256):
                cols = slice(q * 256, (q + 1) * 256)
                product = jnp.dot(lhs[...], lam_v[j, :, cols], preferred_element_type=jnp.float32)
                part[k][j, :, :, cols] = product.reshape(NZ, R, 256)
            return carry

        lax.fori_loop(0, 2, half, 0)
        far = stepz(z, 4)
        send, recv = h_send.at[k, 0], h_recv.at[k, 0]
        for n, d in enumerate((1, -1)):
            remote(part[k].at[n, far], hop0.at[k, n], send, recv, near_z(d)).start()
        expect(hop0.at[k], send, recv, (k, "h0"))
        give = remote(part[k].at[1 - core, z], swap.at[k], s_send.at[k], s_recv.at[k], partner)
        give.start()
        arrivals[k, "swap"] = give
        sent.append(give)

    def near_z(d):
        return dev(x, y, core, stepz(z, d))

    def hop_1(k):
        arrivals[k, "h0"].wait_recv()
        send, recv = h_send.at[k, 1], h_recv.at[k, 1]
        for n, d in enumerate((1, -1)):
            block = stepz(z, 3 * d)
            part[k][n, block] = part[k][n, block] + hop0[k, n]
            remote(part[k].at[:, block], hop1.at[k, n], send, recv, near_z(d)).start()
        expect(hop1.at[k], send, recv, (k, "h1"))

    def hop_2(k):
        arrivals[k, "h1"].wait_recv()
        send, recv = h_send.at[k, 2], h_recv.at[k, 2]
        for n, d in enumerate((1, -1)):
            block = stepz(z, 2 * d)
            part[k][:, block] = part[k][:, block] + hop1[k, n]
            remote(part[k].at[:, block], hop2.at[k, n], send, recv, near_z(d)).start()
        expect(hop2.at[k], send, recv, (k, "h2"))

    def hop_3(k):
        arrivals[k, "h2"].wait_recv()
        send, recv = h_send.at[k, 3], h_recv.at[k, 3]
        for n, d in enumerate((1, -1)):
            block = stepz(z, d)
            for j in (0, 1):
                part[k][j, block] = part[k][j, block] + hop2[k, n, j]
                remote(part[k].at[j, block], last.at[k, n, core], send, recv, updown[d][j]).start()
        expect(last.at[k], send, recv, (k, "h3"))

    def finish(k):
        arrivals[k, "swap"].wait_recv()
        arrivals[k, "h3"].wait_recv()
        for who, own in ((core, part[k][core, z]), (1 - core, swap[k])):
            rows = pl.ds(pl.multiple_of(who * 128 + k * R, R), R)
            ladder = own + last[k, 0, who] + last[k, 1, who]
            v = vir_t[rows, :]
            den = occ_v[...] - jnp.concatenate([v] * (W2 // 128), axis=1)
            out_ref[rows, :] = ((other_v[rows, :].astype(jnp.float32) + ladder) / den).astype(jnp.bfloat16)

    stage_1a(0)
    ids_first()
    give_lam = remote(lam_ref, lam_v.at[core], lam_send, lam_recv, partner)
    give_lam.start()
    sent.append(give_lam)

    run = (stage_1a, stage_1b, stage_2a, stage_2b, multiply, hop_1, hop_2, hop_3, finish)
    table = timetable()
    for step in range(1 + max(step for step, stage in table)):
        if step == 1:
            ids_second()
        for stage in range(9):
            if step == 2 and stage == S_MM:
                ids_done()
            for k in table.get((step, stage), ()):
                if (k, stage) != (0, S_1A):
                    run[stage](k)

    for c in sent:
        c.wait_send()


def body(w_tiles, task_ab, task_ef, lam_pairs, other_terms, vir_pair, occ_pair):
    w = w_tiles.reshape(2, 2, NK, R, TILE)
    anyspace = pl.BlockSpec(memory_space=pl.ANY)
    smem = pl.BlockSpec(memory_space=pltpu.SMEM)
    f32, bf16 = jnp.float32, jnp.bfloat16
    dma = pltpu.SemaphoreType.DMA
    scratch = [pltpu.VMEM((32, 2, R, TILE), bf16) for _ in range(NK)]
    scratch += [pltpu.VMEM((2, NZ, R, W2), f32) for _ in range(NK)]
    scratch += [
        pltpu.VMEM((2, 2, NK, R, TILE), bf16),
        pltpu.VMEM((2, EF_T * TILE, W2), bf16),
        pltpu.VMEM((AB_T * 2 * R, EF_T * TILE), bf16),
        pltpu.VMEM((NK, 2, R, W2), f32),
        pltpu.VMEM((NK, 2, 2, R, W2), f32),
        pltpu.VMEM((NK, 2, 2, R, W2), f32),
        pltpu.VMEM((NK, 2, 2, R, W2), f32),
        pltpu.VMEM((NK, R, W2), f32),
        pltpu.VMEM((256, W2), bf16),
        pltpu.VMEM((2, 128), f32),
        pltpu.VMEM((1, W2), f32),
        pltpu.VMEM((256, 128), f32),
        pltpu.VMEM((32, 8, 128), jnp.int32),
        pltpu.VMEM((8, 128), jnp.int32),
        pltpu.SMEM((8, 128), jnp.int32),
        dma((6,)),
        dma, dma,
        dma((2,)), dma((2,)),
        dma((NK, 4)), dma((NK, 4)),
        dma((NK, 4)), dma((NK, 4)),
        dma((NK,)), dma((NK,)),
    ]
    return pl.pallas_call(
        kernel,
        out_shape=jax.ShapeDtypeStruct((256, W2), bf16),
        in_specs=[smem, smem] + [anyspace] * 5,
        out_specs=pl.BlockSpec(memory_space=pltpu.VMEM),
        scratch_shapes=scratch,
        compiler_params=pltpu.CompilerParams(
            collective_id=0, has_side_effects=True, vmem_limit_bytes=VMEM
        ),
        cost_estimate=pl.CostEstimate(
            flops=2 * 2048 * 4096 * 512, bytes_accessed=6 * 1024 * 1024, transcendentals=0
        ),
    )(task_ab, task_ef, w, lam_pairs, other_terms, vir_pair.reshape(2, 128), occ_pair.reshape(1, W2))


def solution(mesh):
    placed = (
        P(("col", "row"), None, None),
        P(("col", "row")),
        P(("col", "row")),
        P("row", "col"),
        P("row", "col"),
        P("row"),
        P("col"),
    )
    return jax.shard_map(
        body, mesh=mesh, in_specs=placed, out_specs=P("row", "col"), check_vma=False
    )
```

time: 96.2 us -> 89.7 us (0.932)
  local copies, waits for them, and re-layouts: 6.24 us -> 1.67 us
  Pallas kernels: 88.4 us -> 86.7 us
    unnamed x11 -> x1, local copies, waits for them, and re-layouts: 6.24 us -> 1.67 us
    pallas_call x1, Pallas kernels: 88.4 us -> 86.7 us  [body(): pl.pallas_call(kernel, out_shape=jax.ShapeDtypeStruct((256, W2), bf16), i...]
where the time goes in v2:
time: 89.7 us; the launch traced here: 89.6 us
  Pallas kernels  86.7 us (97%)
  local copies, waits for them, and re-layouts  1.67 us (2%)
  between operations  1.3 us (1%)
    pallas_call x1, Pallas kernels, body(): pl.pallas_call(kernel, out_shape=jax.ShapeDtypeStruct((256, W2), bf16), i...  86.7 us

profile of v2, /device:TPU:1, one launch (start us, length us, event | category | flops | bytes accessed | tf_op | source)
XLA Modules:
  0.0 89.6 jit_solution(603386942022767044)
XLA Ops:
  1.3 86.7 %shard_map.73 = bf16[256,512]{1,0:T(8,128)(2,1)} custom-call(s32[1]{0:T(128)S(6)} %copy.9.ab_ref, s32[1]{0:T(128)S(6)} %copy.10.ef_ref, bf16[2,2,8,16,512]{4,3,2,1,0:T(8,128)(2,1)} %bitcast.3, bf16[4096,512]{1,0:T(8,128)(2,1)} %lam_ref.1, bf16[256,512]{1,0:T(8,128)(2,1)} %other_ref.1, f32[2,128]{1,0:T(2,128)} %bitcast.5, f32[1,512]{1,0:T(1,128)} %bitcast.4), custom_call_target="tpu_custom_call" | custom-call | flops 8589934592 | bytes 6291456 | tf_op jit(solution)/shard_map/pallas_call | solution.py:317
  88.0 1.7 %copy.11 = bf16[256,512]{1,0:T(8,128)(2,1)} copy(bf16[256,512]{1,0:T(8,128)(2,1)} %shard_map.73) | data formatting | bytes 524288

commit v3 on v2

--- a/solution.py
+++ b/solution.py
@@ -18,20 +18,14 @@
 S_1A, S_1B, S_2A, S_2B, S_MM, S_H1, S_H2, S_H3, S_FIN = range(9)
 
 
-def timetable():
-    table = {}
-
-    def put(step, stage, k):
-        table.setdefault((step, stage), []).append(k)
-
-    for k in range(NK):
-        if k == 0:
-            times = {S_1A: 0, S_2A: 1, S_MM: 2, S_H1: 3, S_H2: 4, S_H3: 5, S_FIN: 6}
-        else:
-            times = {stage: k - 1 + stage for stage in range(9)}
-        for stage, step in times.items():
-            put(step, stage, k)
-    return table
+ORDER = (
+     2,  0,  1,  4,  5, 12,  6,  3, 11, 10, 14, 22, 20, 32, 21, 24,
+    30, 42,  7, 15, 31, 52, 13, 34, 16, 40, 25, 62, 41, 17, 23, 44,
+    50, 51, 35, 26, 54, 27, 72, 61, 45, 60, 33, 36, 64, 71, 37, 55,
+    70, 43, 74, 46, 47, 65, 81, 53, 56, 57, 75, 63, 66, 67, 82, 73,
+    80, 76, 77, 83, 86, 84, 85, 87,
+)
+DIRECT = ()
 
 
 def kernel(ab_ref, ef_ref, w_ref, lam_ref, other_ref, vir_ref, occ_ref, out_ref, *scratch):
@@ -100,7 +94,7 @@
     my_slot = core * 16 + jnp.where(core == 0, y * 4 + x, x * 4 + y)
     my_id = (y * 4 + x) * 2 + core
     code = ab_ref[0] * EF_T + ef_ref[0]
-    lane = lax.broadcasted_iota(jnp.int32, (8, 128), 1)
+    lane = lax.broadcasted_iota(jnp.int32, (1, 128), 1)
     ids[my_id] = jnp.where(lane == code, my_slot, 0)
     get_w.wait()
     for k in range(NK):
@@ -117,7 +111,7 @@
 
     def stage_1a(k):
         send, recv = g_send.at[k, 0], g_recv.at[k, 0]
-        hops = (1, -1, 2) if k == 0 else (1, -1)
+        hops = (1, -1, 2) if k in DIRECT else (1, -1)
         for d in hops:
             for j in (0, 1):
                 remote(w_v.at[:, j, k], land[k].at[my_slot], send, recv, mine_along(d, j)).start()
@@ -144,9 +138,9 @@
         expect(land[k].at[pl.ds(0, 2)], send, recv, (k, 1))
 
     def stage_2a(k):
-        arrivals[k, 0 if k == 0 else 1].wait_recv()
+        arrivals[k, 0 if k in DIRECT else 1].wait_recv()
         send, recv = g_send.at[k, 2], g_recv.at[k, 2]
-        hops = (1, -1, 2) if k == 0 else (1, -1)
+        hops = (1, -1, 2) if k in DIRECT else (1, -1)
         for g in (0, 1):
             view = land[k].at[pl.ds(slot(g, second[g], 0), 4)]
             for d in hops:
@@ -191,7 +185,7 @@
         give_lam.wait_recv()
 
     def multiply(k):
-        arrivals[k, 2 if k == 0 else 3].wait_recv()
+        arrivals[k, 2 if k in DIRECT else 3].wait_recv()
 
         def order(ab, carry):
             for ef in range(EF_T):
@@ -261,23 +255,22 @@
             den = occ_v[...] - jnp.concatenate([v] * (W2 // 128), axis=1)
             out_ref[rows, :] = ((other_v[rows, :].astype(jnp.float32) + ladder) / den).astype(jnp.bfloat16)
 
-    stage_1a(0)
+    stage_1a(ORDER[0])
     ids_first()
     give_lam = remote(lam_ref, lam_v.at[core], lam_send, lam_recv, partner)
     give_lam.start()
     sent.append(give_lam)
 
     run = (stage_1a, stage_1b, stage_2a, stage_2b, multiply, hop_1, hop_2, hop_3, finish)
-    table = timetable()
-    for step in range(1 + max(step for step, stage in table)):
-        if step == 1:
+    first_2a = next(n for n, item in enumerate(ORDER) if item // 10 == S_2A)
+    first_mm = next(n for n, item in enumerate(ORDER) if item // 10 == S_MM)
+    for n, item in enumerate(ORDER):
+        if n == first_2a:
             ids_second()
-        for stage in range(9):
-            if step == 2 and stage == S_MM:
-                ids_done()
-            for k in table.get((step, stage), ()):
-                if (k, stage) != (0, S_1A):
-                    run[stage](k)
+        if n == first_mm:
+            ids_done()
+        if n > 0:
+            run[item // 10](item % 10)
 
     for c in sent:
         c.wait_send()
@@ -304,9 +297,9 @@
         pltpu.VMEM((2, 128), f32),
         pltpu.VMEM((1, W2), f32),
         pltpu.VMEM((256, 128), f32),
-        pltpu.VMEM((32, 8, 128), jnp.int32),
-        pltpu.VMEM((8, 128), jnp.int32),
-        pltpu.SMEM((8, 128), jnp.int32),
+        pltpu.VMEM((32, 1, 128), jnp.int32),
+        pltpu.VMEM((1, 128), jnp.int32),
+        pltpu.SMEM((1, 128), jnp.int32),
         dma((6,)),
         dma, dma,
         dma((2,)), dma((2,)),

time: 89.7 us -> 82.6 us (0.921)
  Pallas kernels: 86.7 us -> 79.5 us
    pallas_call x1, Pallas kernels: 86.7 us -> 79.5 us  [body(): pl.pallas_call(kernel, out_shape=jax.ShapeDtypeStruct((256, W2), bf16), i...]
where the time goes in v3:
time: 82.6 us; the launch traced here: 82.4 us
  Pallas kernels  79.5 us (96%)
  local copies, waits for them, and re-layouts  1.67 us (2%)
  between operations  1.3 us (2%)
    pallas_call x1, Pallas kernels, body(): pl.pallas_call(kernel, out_shape=jax.ShapeDtypeStruct((256, W2), bf16), i...  79.5 us
    unnamed x1, local copies, waits for them, and re-layouts  1.67 us

profile of v3, /device:TPU:1, one launch (start us, length us, event | category | flops | bytes accessed | tf_op | source)
XLA Modules:
  0.0 82.4 jit_solution(4448011127339437649)
XLA Ops:
  1.3 79.5 %shard_map.73 = bf16[256,512]{1,0:T(8,128)(2,1)} custom-call(s32[1]{0:T(128)S(6)} %copy.9.ab_ref, s32[1]{0:T(128)S(6)} %copy.10.ef_ref, bf16[2,2,8,16,512]{4,3,2,1,0:T(8,128)(2,1)} %bitcast.3, bf16[4096,512]{1,0:T(8,128)(2,1)} %lam_ref.1, bf16[256,512]{1,0:T(8,128)(2,1)} %other_ref.1, f32[2,128]{1,0:T(2,128)} %bitcast.5, f32[1,512]{1,0:T(1,128)} %bitcast.4), custom_call_target="tpu_custom_call" | custom-call | flops 8589934592 | bytes 6291456 | tf_op jit(solution)/shard_map/pallas_call | solution.py:310
  80.8 1.7 %copy.11 = bf16[256,512]{1,0:T(8,128)(2,1)} copy(bf16[256,512]{1,0:T(8,128)(2,1)} %shard_map.73) | data formatting | bytes 524288

commit v4 on v3

--- a/solution.py
+++ b/solution.py
@@ -19,20 +19,42 @@
 
 
 ORDER = (
-     2,  0,  1,  4,  5, 12,  6,  3, 11, 10, 14, 22, 20, 32, 21, 24,
-    30, 42,  7, 15, 31, 52, 13, 34, 16, 40, 25, 62, 41, 17, 23, 44,
-    50, 51, 35, 26, 54, 27, 72, 61, 45, 60, 33, 36, 64, 71, 37, 55,
-    70, 43, 74, 46, 47, 65, 81, 53, 56, 57, 75, 63, 66, 67, 82, 73,
-    80, 76, 77, 83, 86, 84, 85, 87,
+     2,  4,  1,  5,  3, 12,  0, 14,  6, 11,  7, 15, 22, 21, 17, 24,
+    16, 13, 31, 10, 32, 23, 34, 25, 41, 42, 33, 51, 20, 52, 44, 35,
+    61, 26, 43, 62, 30, 54, 27, 71, 45, 53, 64, 36, 72, 40, 55, 63,
+    37, 74, 46, 50, 65, 47, 56, 84, 60, 57, 66, 75, 67, 73, 81, 82,
+    70, 76, 77, 80, 85, 83, 86, 87,
 )
 DIRECT = ()
+
+
+def split(v):
+    high = v.astype(jnp.bfloat16)
+    wide = high.astype(jnp.float32)
+    most = jnp.max(jnp.abs(wide), axis=0, keepdims=True)
+    scale = jnp.where(most > 1e-33, 32512.0 / most, 0.0)
+    u = ((v - wide) * scale + 128.5).astype(jnp.int32)
+    low = u[:, 384:]
+    for part, bits in ((u[:, :128], 24), (u[:, 128:256], 16), (u[:, 256:384], 8)):
+        low = low | lax.shift_left(part, jnp.full(part.shape, bits, jnp.int32))
+    return high, low
+
+
+def join(high, low):
+    wide = high.astype(jnp.float32)
+    most = jnp.max(jnp.abs(wide), axis=0, keepdims=True)
+    parts = [
+        lax.shift_right_logical(low, jnp.full(low.shape, bits, jnp.int32)) & 255 for bits in (24, 16, 8)
+    ] + [low & 255]
+    u = jnp.concatenate(parts, axis=1)
+    return wide + (u - 128).astype(jnp.float32) * (most * (1.0 / 32512.0))
 
 
 def kernel(ab_ref, ef_ref, w_ref, lam_ref, other_ref, vir_ref, occ_ref, out_ref, *scratch):
     land = scratch[:NK]
     part = scratch[NK : 2 * NK]
     (
-        w_v, lam_v, lhs, hop0, hop1, hop2, last, swap, other_v, vir_v, occ_v, vir_t,
+        w_v, lam_v, lhs, hop0, hop1, hop2, last, low0, low1, low2, lowl, out0, outs, lout0, louts, swap, other_v, vir_v, occ_v, vir_t,
         ids, inv_v, inv_s,
         in_sem, lam_send, lam_recv, id_send, id_recv, g_send, g_recv,
         h_send, h_recv, s_send, s_recv,
@@ -205,10 +227,10 @@
 
         lax.fori_loop(0, 2, half, 0)
         far = stepz(z, 4)
-        send, recv = h_send.at[k, 0], h_recv.at[k, 0]
         for n, d in enumerate((1, -1)):
-            remote(part[k].at[n, far], hop0.at[k, n], send, recv, near_z(d)).start()
-        expect(hop0.at[k], send, recv, (k, "h0"))
+            out0[k, n], lout0[k, n] = split(part[k][n, far])
+            ship(k, 0, out0.at[k, n], lout0.at[k, n], hop0.at[k, n], low0.at[k, n], near_z(d))
+        expect_both(k, 0, hop0.at[k], low0.at[k])
         give = remote(part[k].at[1 - core, z], swap.at[k], s_send.at[k], s_recv.at[k], partner)
         give.start()
         arrivals[k, "swap"] = give
@@ -217,40 +239,59 @@
     def near_z(d):
         return dev(x, y, core, stepz(z, d))
 
+    def ship(k, stage, high, low, high_to, low_to, who):
+        remote(high, high_to, h_send.at[k, stage, 0], h_recv.at[k, stage, 0], who).start()
+        remote(low, low_to, h_send.at[k, stage, 1], h_recv.at[k, stage, 1], who).start()
+
+    def expect_both(k, stage, high, low):
+        expect(high, h_send.at[k, stage, 0], h_recv.at[k, stage, 0], (k, "high", stage))
+        expect(low, h_send.at[k, stage, 1], h_recv.at[k, stage, 1], (k, "low", stage))
+
+    def arrived(k, stage):
+        arrivals[k, "high", stage].wait_recv()
+        arrivals[k, "low", stage].wait_recv()
+
     def hop_1(k):
-        arrivals[k, "h0"].wait_recv()
-        send, recv = h_send.at[k, 1], h_recv.at[k, 1]
+        arrived(k, 0)
         for n, d in enumerate((1, -1)):
             block = stepz(z, 3 * d)
-            part[k][n, block] = part[k][n, block] + hop0[k, n]
-            remote(part[k].at[:, block], hop1.at[k, n], send, recv, near_z(d)).start()
-        expect(hop1.at[k], send, recv, (k, "h1"))
+            for j in (0, 1):
+                v = part[k][j, block]
+                if j == n:
+                    v = v + join(hop0[k, n], low0[k, n])
+                outs[k, 0, n, j], louts[k, 0, n, j] = split(v)
+            ship(k, 1, outs.at[k, 0, n], louts.at[k, 0, n], hop1.at[k, n], low1.at[k, n], near_z(d))
+        expect_both(k, 1, hop1.at[k], low1.at[k])
 
     def hop_2(k):
-        arrivals[k, "h1"].wait_recv()
-        send, recv = h_send.at[k, 2], h_recv.at[k, 2]
+        arrived(k, 1)
         for n, d in enumerate((1, -1)):
             block = stepz(z, 2 * d)
-            part[k][:, block] = part[k][:, block] + hop1[k, n]
-            remote(part[k].at[:, block], hop2.at[k, n], send, recv, near_z(d)).start()
-        expect(hop2.at[k], send, recv, (k, "h2"))
+            for j in (0, 1):
+                v = part[k][j, block] + join(hop1[k, n, j], low1[k, n, j])
+                outs[k, 1, n, j], louts[k, 1, n, j] = split(v)
+            ship(k, 2, outs.at[k, 1, n], louts.at[k, 1, n], hop2.at[k, n], low2.at[k, n], near_z(d))
+        expect_both(k, 2, hop2.at[k], low2.at[k])
 
     def hop_3(k):
-        arrivals[k, "h2"].wait_recv()
-        send, recv = h_send.at[k, 3], h_recv.at[k, 3]
+        arrived(k, 2)
         for n, d in enumerate((1, -1)):
             block = stepz(z, d)
             for j in (0, 1):
-                part[k][j, block] = part[k][j, block] + hop2[k, n, j]
-                remote(part[k].at[j, block], last.at[k, n, core], send, recv, updown[d][j]).start()
-        expect(last.at[k], send, recv, (k, "h3"))
+                v = part[k][j, block] + join(hop2[k, n, j], low2[k, n, j])
+                outs[k, 2, n, j], louts[k, 2, n, j] = split(v)
+                ship(
+                    k, 3, outs.at[k, 2, n, j], louts.at[k, 2, n, j],
+                    last.at[k, n, core], lowl.at[k, n, core], updown[d][j],
+                )
+        expect_both(k, 3, last.at[k], lowl.at[k])
 
     def finish(k):
         arrivals[k, "swap"].wait_recv()
-        arrivals[k, "h3"].wait_recv()
+        arrived(k, 3)
         for who, own in ((core, part[k][core, z]), (1 - core, swap[k])):
             rows = pl.ds(pl.multiple_of(who * 128 + k * R, R), R)
-            ladder = own + last[k, 0, who] + last[k, 1, who]
+            ladder = own + join(last[k, 0, who], lowl[k, 0, who]) + join(last[k, 1, who], lowl[k, 1, who])
             v = vir_t[rows, :]
             den = occ_v[...] - jnp.concatenate([v] * (W2 // 128), axis=1)
             out_ref[rows, :] = ((other_v[rows, :].astype(jnp.float32) + ladder) / den).astype(jnp.bfloat16)
@@ -288,10 +329,18 @@
         pltpu.VMEM((2, 2, NK, R, TILE), bf16),
         pltpu.VMEM((2, EF_T * TILE, W2), bf16),
         pltpu.VMEM((AB_T * 2 * R, EF_T * TILE), bf16),
-        pltpu.VMEM((NK, 2, R, W2), f32),
-        pltpu.VMEM((NK, 2, 2, R, W2), f32),
-        pltpu.VMEM((NK, 2, 2, R, W2), f32),
-        pltpu.VMEM((NK, 2, 2, R, W2), f32),
+        pltpu.VMEM((NK, 2, R, W2), bf16),
+        pltpu.VMEM((NK, 2, 2, R, W2), bf16),
+        pltpu.VMEM((NK, 2, 2, R, W2), bf16),
+        pltpu.VMEM((NK, 2, 2, R, W2), bf16),
+        pltpu.VMEM((NK, 2, R, 128), jnp.int32),
+        pltpu.VMEM((NK, 2, 2, R, 128), jnp.int32),
+        pltpu.VMEM((NK, 2, 2, R, 128), jnp.int32),
+        pltpu.VMEM((NK, 2, 2, R, 128), jnp.int32),
+        pltpu.VMEM((NK, 2, R, W2), bf16),
+        pltpu.VMEM((NK, 3, 2, 2, R, W2), bf16),
+        pltpu.VMEM((NK, 2, R, 128), jnp.int32),
+        pltpu.VMEM((NK, 3, 2, 2, R, 128), jnp.int32),
         pltpu.VMEM((NK, R, W2), f32),
         pltpu.VMEM((256, W2), bf16),
         pltpu.VMEM((2, 128), f32),
@@ -304,7 +353,7 @@
         dma, dma,
         dma((2,)), dma((2,)),
         dma((NK, 4)), dma((NK, 4)),
-        dma((NK, 4)), dma((NK, 4)),
+        dma((NK, 4, 2)), dma((NK, 4, 2)),
         dma((NK,)), dma((NK,)),
     ]
     return pl.pallas_call(

time: 82.6 us -> 79.4 us (0.961)
  Pallas kernels: 79.5 us -> 76.4 us
    pallas_call x1, Pallas kernels: 79.5 us -> 76.4 us  [body(): pl.pallas_call(kernel, out_shape=jax.ShapeDtypeStruct((256, W2), bf16), i...]
where the time goes in v4:
time: 79.4 us; the launch traced here: 79.3 us
  Pallas kernels  76.4 us (96%)
  local copies, waits for them, and re-layouts  1.67 us (2%)
  between operations  1.3 us (2%)
    pallas_call x1, Pallas kernels, body(): pl.pallas_call(kernel, out_shape=jax.ShapeDtypeStruct((256, W2), bf16), i...  76.4 us
    unnamed x1, local copies, waits for them, and re-layouts  1.67 us

profile of v4, /device:TPU:1, one launch (start us, length us, event | category | flops | bytes accessed | tf_op | source)
XLA Modules:
  0.0 79.3 jit_solution(15625330081748369844)
XLA Ops:
  1.3 76.4 %shard_map.73 = bf16[256,512]{1,0:T(8,128)(2,1)} custom-call(s32[1]{0:T(128)S(6)} %copy.9.ab_ref, s32[1]{0:T(128)S(6)} %copy.10.ef_ref, bf16[2,2,8,16,512]{4,3,2,1,0:T(8,128)(2,1)} %bitcast.3, bf16[4096,512]{1,0:T(8,128)(2,1)} %lam_ref.1, bf16[256,512]{1,0:T(8,128)(2,1)} %other_ref.1, f32[2,128]{1,0:T(2,128)} %bitcast.5, f32[1,512]{1,0:T(1,128)} %bitcast.4), custom_call_target="tpu_custom_call" | custom-call | flops 8589934592 | bytes 6291456 | tf_op jit(solution)/shard_map/pallas_call | solution.py:359
  77.7 1.7 %copy.11 = bf16[256,512]{1,0:T(8,128)(2,1)} copy(bf16[256,512]{1,0:T(8,128)(2,1)} %shard_map.73) | data formatting | bytes 524288

commit v5 on v4

--- a/solution.py
+++ b/solution.py
@@ -13,7 +13,7 @@
 NK = 8
 R = 16
 W2 = 512
-VMEM = 63 * 1024 * 1024
+VMEM = 54784 * 1024
 
 S_1A, S_1B, S_2A, S_2B, S_MM, S_H1, S_H2, S_H3, S_FIN = range(9)
 
@@ -56,8 +56,7 @@
     (
         w_v, lam_v, lhs, hop0, hop1, hop2, last, low0, low1, low2, lowl, out0, outs, lout0, louts, swap, other_v, vir_v, occ_v, vir_t,
         ids, inv_v, inv_s,
-        in_sem, lam_send, lam_recv, id_send, id_recv, g_send, g_recv,
-        h_send, h_recv, s_send, s_recv,
+        in_sem, lam_send, lam_recv, id_send, id_recv, c_send, g_recv, h_recv, s_recv,
     ) = scratch[2 * NK :]
 
     col = lax.axis_index("col")
@@ -124,15 +123,13 @@
 
     pl.semaphore_wait(barrier, len(greeted))
 
-    sent = []
-
     def mine_along(d, j):
         xx = jnp.where(core == 0, step4(x, d), x)
         yy = jnp.where(core == 0, y, step4(y, d))
         return dev(xx, yy, j, z)
 
     def stage_1a(k):
-        send, recv = g_send.at[k, 0], g_recv.at[k, 0]
+        send, recv = c_send.at[k], g_recv.at[k, 0]
         hops = (1, -1, 2) if k in DIRECT else (1, -1)
         for d in hops:
             for j in (0, 1):
@@ -143,16 +140,14 @@
     arrivals = {}
 
     def expect(view, send, recv, key):
-        both = remote(view, view, send, recv, partner)
-        arrivals[key] = both
-        sent.append(both)
+        arrivals[key] = remote(view, view, send, recv, partner)
 
     def slot(g, s, p):
         return g * 16 + s * 4 + p
 
     def stage_1b(k):
         arrivals[k, 0].wait_recv()
-        send, recv = g_send.at[k, 1], g_recv.at[k, 1]
+        send, recv = c_send.at[k], g_recv.at[k, 1]
         for g in (0, 1):
             for n, d in enumerate((1, -1)):
                 view = land[k].at[slot(g, second[g], step4(prime[g], -d)), n]
@@ -161,7 +156,7 @@
 
     def stage_2a(k):
         arrivals[k, 0 if k in DIRECT else 1].wait_recv()
-        send, recv = g_send.at[k, 2], g_recv.at[k, 2]
+        send, recv = c_send.at[k], g_recv.at[k, 2]
         hops = (1, -1, 2) if k in DIRECT else (1, -1)
         for g in (0, 1):
             view = land[k].at[pl.ds(slot(g, second[g], 0), 4)]
@@ -171,7 +166,7 @@
 
     def stage_2b(k):
         arrivals[k, 2].wait_recv()
-        send, recv = g_send.at[k, 3], g_recv.at[k, 3]
+        send, recv = c_send.at[k], g_recv.at[k, 3]
         for g in (0, 1):
             for n, d in enumerate((1, -1)):
                 view = land[k].at[pl.ds(slot(g, step4(second[g], -d), 2 * n), 2)]
@@ -230,26 +225,23 @@
         for n, d in enumerate((1, -1)):
             out0[k, n], lout0[k, n] = split(part[k][n, far])
             ship(k, 0, out0.at[k, n], lout0.at[k, n], hop0.at[k, n], low0.at[k, n], near_z(d))
-        expect_both(k, 0, hop0.at[k], low0.at[k])
-        give = remote(part[k].at[1 - core, z], swap.at[k], s_send.at[k], s_recv.at[k], partner)
+        expect_hop(k, 0)
+        give = remote(part[k].at[1 - core, z], swap.at[k], c_send.at[k], s_recv.at[k], partner)
         give.start()
         arrivals[k, "swap"] = give
-        sent.append(give)
 
     def near_z(d):
         return dev(x, y, core, stepz(z, d))
 
     def ship(k, stage, high, low, high_to, low_to, who):
-        remote(high, high_to, h_send.at[k, stage, 0], h_recv.at[k, stage, 0], who).start()
-        remote(low, low_to, h_send.at[k, stage, 1], h_recv.at[k, stage, 1], who).start()
-
-    def expect_both(k, stage, high, low):
-        expect(high, h_send.at[k, stage, 0], h_recv.at[k, stage, 0], (k, "high", stage))
-        expect(low, h_send.at[k, stage, 1], h_recv.at[k, stage, 1], (k, "low", stage))
+        remote(high, high_to, c_send.at[k], h_recv.at[k, stage], who).start()
+        remote(low, low_to, c_send.at[k], h_recv.at[k, stage], who).start()
+
+    def expect_hop(k, stage):
+        expect(lam_v.at[0, pl.ds(0, 48 if stage == 0 else 96)], c_send.at[k], h_recv.at[k, stage], (k, "hop", stage))
 
     def arrived(k, stage):
-        arrivals[k, "high", stage].wait_recv()
-        arrivals[k, "low", stage].wait_recv()
+        arrivals[k, "hop", stage].wait_recv()
 
     def hop_1(k):
         arrived(k, 0)
@@ -261,7 +253,7 @@
                     v = v + join(hop0[k, n], low0[k, n])
                 outs[k, 0, n, j], louts[k, 0, n, j] = split(v)
             ship(k, 1, outs.at[k, 0, n], louts.at[k, 0, n], hop1.at[k, n], low1.at[k, n], near_z(d))
-        expect_both(k, 1, hop1.at[k], low1.at[k])
+        expect_hop(k, 1)
 
     def hop_2(k):
         arrived(k, 1)
@@ -271,7 +263,7 @@
                 v = part[k][j, block] + join(hop1[k, n, j], low1[k, n, j])
                 outs[k, 1, n, j], louts[k, 1, n, j] = split(v)
             ship(k, 2, outs.at[k, 1, n], louts.at[k, 1, n], hop2.at[k, n], low2.at[k, n], near_z(d))
-        expect_both(k, 2, hop2.at[k], low2.at[k])
+        expect_hop(k, 2)
 
     def hop_3(k):
         arrived(k, 2)
@@ -284,7 +276,7 @@
                     k, 3, outs.at[k, 2, n, j], louts.at[k, 2, n, j],
                     last.at[k, n, core], lowl.at[k, n, core], updown[d][j],
                 )
-        expect_both(k, 3, last.at[k], lowl.at[k])
+        expect_hop(k, 3)
 
     def finish(k):
         arrivals[k, "swap"].wait_recv()
@@ -300,7 +292,6 @@
     ids_first()
     give_lam = remote(lam_ref, lam_v.at[core], lam_send, lam_recv, partner)
     give_lam.start()
-    sent.append(give_lam)
 
     run = (stage_1a, stage_1b, stage_2a, stage_2b, multiply, hop_1, hop_2, hop_3, finish)
     first_2a = next(n for n, item in enumerate(ORDER) if item // 10 == S_2A)
@@ -313,8 +304,14 @@
         if n > 0:
             run[item // 10](item % 10)
 
-    for c in sent:
-        c.wait_send()
+    for key in ("id0", "id1"):
+        arrivals[key].wait_send()
+    give_lam.wait_send()
+    for k in range(NK):
+        first = 7 * 32 if k in DIRECT else 5 * 32
+        plane = first + (24 * 32 if k in DIRECT else 64 + 512 + 256)
+        view = lam_v.at[0, pl.ds(0, plane + 48 + 3 * 96 + 32)]
+        remote(view, view, c_send.at[k], s_recv.at[k], partner).wait_send()
 
 
 def body(w_tiles, task_ab, task_ef, lam_pairs, other_terms, vir_pair, occ_pair):
@@ -352,9 +349,8 @@
         dma((6,)),
         dma, dma,
         dma((2,)), dma((2,)),
-        dma((NK, 4)), dma((NK, 4)),
-        dma((NK, 4, 2)), dma((NK, 4, 2)),
-        dma((NK,)), dma((NK,)),
+        dma((NK,)), dma((NK, 4)),
+        dma((NK, 4)), dma((NK,)),
     ]
     return pl.pallas_call(
         kernel,

time: 79.4 us -> 77.6 us (0.977)
  Pallas kernels: 76.4 us -> 74.1 us
    pallas_call x1, Pallas kernels: 76.4 us -> 74.1 us  [body(): pl.pallas_call(kernel, out_shape=jax.ShapeDtypeStruct((256, W2), bf16), i...]
    unnamed x1 -> x5, local copies, waits for them, and re-layouts: 1.67 us -> 2.06 us
where the time goes in v5:
time: 77.6 us; the launch traced here: 77.5 us
  Pallas kernels  74.1 us (95%)
  local copies, waits for them, and re-layouts  2.06 us (3%)
  between operations  1.31 us (2%)
    pallas_call x1, Pallas kernels, body(): pl.pallas_call(kernel, out_shape=jax.ShapeDtypeStruct((256, W2), bf16), i...  74.1 us
    unnamed x5, local copies, waits for them, and re-layouts  2.06 us

profile of v5, /device:TPU:1, one launch (start us, length us, event | category | flops | bytes accessed | tf_op | source)
XLA Modules:
  0.0 77.5 jit_solution(4652315784936168711)
XLA Ops:
  1.3 0.0 copy-start
  1.3 0.7 copy-done
  2.0 0.0 copy-start.1
  2.0 0.7 copy-done.1
  2.7 74.1 %shard_map.73 = bf16[256,512]{1,0:T(8,128)(2,1)S(1)} custom-call(s32[1]{0:T(128)S(6)} %copy.9.ab_ref, s32[1]{0:T(128)S(6)} %copy.10.ef_ref, bf16[2,2,8,16,512]{4,3,2,1,0:T(8,128)(2,1)} %bitcast.5, bf16[4096,512]{1,0:T(8,128)(2,1)} %lam_ref.1, bf16[256,512]{1,0:T(8,128)(2,1)} %other_ref.1, f32[2,128]{1,0:T(2,128)S(1)} %bitcast.4, f32[1,512]{1,0:T(1,128)S(1)} %bitcast.3), custom_call_target="tpu_custom_call" | custom-call | flops 8589934592 | bytes 6291456 | tf_op jit(solution)/shard_map/pallas_call | solution.py:355
  76.8 0.7 copy.11
Async XLA Ops:
  1.3 0.7 copy-start
  2.0 0.7 copy-start.1

commit v6 on v5

--- a/solution.py
+++ b/solution.py
@@ -291,7 +291,6 @@
     stage_1a(ORDER[0])
     ids_first()
     give_lam = remote(lam_ref, lam_v.at[core], lam_send, lam_recv, partner)
-    give_lam.start()
 
     run = (stage_1a, stage_1b, stage_2a, stage_2b, multiply, hop_1, hop_2, hop_3, finish)
     first_2a = next(n for n, item in enumerate(ORDER) if item // 10 == S_2A)
@@ -299,6 +298,7 @@
     for n, item in enumerate(ORDER):
         if n == first_2a:
             ids_second()
+            give_lam.start()
         if n == first_mm:
             ids_done()
         if n > 0:

time: 77.6 us -> 77.6 us (level)
  no operation moved by 1% of the time
where the time goes in v6:
time: 77.6 us; the launch traced here: 77.5 us
  Pallas kernels  74.1 us (95%)
  local copies, waits for them, and re-layouts  2.06 us (3%)
  between operations  1.31 us (2%)
    pallas_call x1, Pallas kernels, body(): pl.pallas_call(kernel, out_shape=jax.ShapeDtypeStruct((256, W2), bf16), i...  74.1 us
    unnamed x5, local copies, waits for them, and re-layouts  2.06 us

profile of v6, /device:TPU:1, one launch (start us, length us, event | category | flops | bytes accessed | tf_op | source)
XLA Modules:
  0.0 77.5 jit_solution(8885943426149108681)
XLA Ops:
  1.3 0.0 copy-start
  1.3 0.7 copy-done
  2.0 0.0 copy-start.1
  2.0 0.7 copy-done.1
  2.7 74.1 %shard_map.73 = bf16[256,512]{1,0:T(8,128)(2,1)S(1)} custom-call(s32[1]{0:T(128)S(6)} %copy.9.ab_ref, s32[1]{0:T(128)S(6)} %copy.10.ef_ref, bf16[2,2,8,16,512]{4,3,2,1,0:T(8,128)(2,1)} %bitcast.5, bf16[4096,512]{1,0:T(8,128)(2,1)} %lam_ref.1, bf16[256,512]{1,0:T(8,128)(2,1)} %other_ref.1, f32[2,128]{1,0:T(2,128)S(1)} %bitcast.4, f32[1,512]{1,0:T(1,128)S(1)} %bitcast.3), custom_call_target="tpu_custom_call" | custom-call | flops 8589934592 | bytes 6291456 | tf_op jit(solution)/shard_map/pallas_call | solution.py:355
  76.8 0.7 copy.11
Async XLA Ops:
  1.3 0.7 copy-start
  2.0 0.7 copy-start.1

commit v7 on v6

--- a/solution.py
+++ b/solution.py
@@ -19,11 +19,11 @@
 
 
 ORDER = (
-     2,  4,  1,  5,  3, 12,  0, 14,  6, 11,  7, 15, 22, 21, 17, 24,
-    16, 13, 31, 10, 32, 23, 34, 25, 41, 42, 33, 51, 20, 52, 44, 35,
-    61, 26, 43, 62, 30, 54, 27, 71, 45, 53, 64, 36, 72, 40, 55, 63,
-    37, 74, 46, 50, 65, 47, 56, 84, 60, 57, 66, 75, 67, 73, 81, 82,
-    70, 76, 77, 80, 85, 83, 86, 87,
+     3,  5,  2,  1,  7,  4, 13,  0, 15,  6, 11, 12, 14, 23, 22, 21,
+    24, 33, 31, 32, 34, 10, 25, 16, 43, 41, 17, 42, 20, 53, 44, 35,
+    51, 52, 26, 63, 27, 54, 61, 45, 62, 73, 36, 30, 55, 64, 37, 71,
+    72, 46, 40, 65, 47, 74, 56, 83, 82, 50, 57, 75, 66, 60, 67, 85,
+    76, 70, 84, 77, 81, 80, 86, 87,
 )
 DIRECT = ()
 

time: 77.6 us -> 78 us (level)
  no operation moved by 1% of the time
where the time goes in v7:
time: 78 us; the launch traced here: 77.9 us
  Pallas kernels  74.5 us (96%)
  local copies, waits for them, and re-layouts  2.06 us (3%)
  between operations  1.31 us (2%)
    pallas_call x1, Pallas kernels, body(): pl.pallas_call(kernel, out_shape=jax.ShapeDtypeStruct((256, W2), bf16), i...  74.5 us
    unnamed x5, local copies, waits for them, and re-layouts  2.06 us

profile of v7, /device:TPU:1, one launch (start us, length us, event | category | flops | bytes accessed | tf_op | source)
XLA Modules:
  0.0 77.9 jit_solution(8438516122436460505)
XLA Ops:
  1.3 0.0 copy-start
  1.3 0.7 copy-done
  2.0 0.0 copy-start.1
  2.0 0.7 copy-done.1
  2.7 74.5 %shard_map.73 = bf16[256,512]{1,0:T(8,128)(2,1)S(1)} custom-call(s32[1]{0:T(128)S(6)} %copy.9.ab_ref, s32[1]{0:T(128)S(6)} %copy.10.ef_ref, bf16[2,2,8,16,512]{4,3,2,1,0:T(8,128)(2,1)} %bitcast.5, bf16[4096,512]{1,0:T(8,128)(2,1)} %lam_ref.1, bf16[256,512]{1,0:T(8,128)(2,1)} %other_ref.1, f32[2,128]{1,0:T(2,128)S(1)} %bitcast.4, f32[1,512]{1,0:T(1,128)S(1)} %bitcast.3), custom_call_target="tpu_custom_call" | custom-call | flops 8589934592 | bytes 6291456 | tf_op jit(solution)/shard_map/pallas_call | solution.py:355
  77.2 0.7 copy.11
Async XLA Ops:
  1.3 0.7 copy-start
  2.0 0.7 copy-start.1
